TPU v7x, 256 devices: a whole 4x4x8 slice. The times are simulated.
256 devices in a mesh: seq: 32 (over y_hi, z, core), tp: 8 (over x, y_lo).
Axes of the slice: x: 4, y: 4 (y_hi: 2, y_lo: 2; y = y_hi * 2 + y_lo), z: 8, core: 2. Of those that a mesh axis runs over, the one named last changes fastest.
Arguments:
- hidden: bfloat16 [4096, 7168], P('seq', 'tp'), may hold values from -6 to 6
- w_kv_down: bfloat16 [7168, 576], P('tp'), may hold values from -0.0625 to 0.0625
- kv_gain: float32 [512], replicated, may hold values from 0.1 to 1.9
- q_latent: bfloat16 [4096, 64, 512], P('seq', 'tp'), may hold values from -300 to 300
- q_rope: bfloat16 [4096, 4096], P('seq', 'tp'), may hold values from -6 to 6
- w_value: bfloat16 [64, 512, 128], P('tp'), may hold values from -0.75 to 0.75
Outputs:
- attended: bfloat16 [4096, 8192], P('seq', 'tp')
All inputs are finite; a program needn't handle non-finite values.
Results may differ from a plain program's by a relative error of at most 0.0097.
Values may be sent and summed in bfloat16 or wider, within the bound.
A program may use at most 64 MiB of HBM per device.

v0:
```python
import jax
import jax.numpy as jnp
from jax import lax
from jax.sharding import PartitionSpec as P

KV_RANK = 512
ROPE = 64
SCORE_SCALE = 192.0 ** (-0.5)
ROPE_BASE = 10000.0
EPSILON = 1e-06


def from_everyone(shard, axis):
    size = lax.axis_size(axis)
    return lax.all_to_all(
        jnp.broadcast_to(shard[None], (size, *shard.shape)), axis, 0, 0, tiled=True
    )


def of_everyone(shard, axis):
    everything = from_everyone(shard, axis)
    return jnp.sum(everything, axis=0)


def rotate(values, positions):
    full_width = values.shape[-1]
    half_width = full_width // 2
    frequency = ROPE_BASE ** (-jnp.arange(half_width, dtype=jnp.float32) * 2.0 / full_width)
    angles = positions.astype(jnp.float32)[:, None] * frequency[None, :]
    angle_shape = (angles.shape[0],) + (1,) * (values.ndim - 2) + (half_width,)
    cosine = jnp.cos(angles).reshape(angle_shape)
    sine_part = jnp.sin(angles).reshape(angle_shape)
    first_half = values[..., :half_width]
    second_half = values[..., half_width:]
    return jnp.concatenate(
        [
            first_half * cosine - second_half * sine_part,
            first_half * sine_part + second_half * cosine,
        ],
        -1,
    )


def finish(projection, kv_gain, positions):
    latent_part = projection[:, :KV_RANK]
    mean_square = jnp.mean(latent_part * latent_part, axis=-1, keepdims=True)
    normed = latent_part * lax.rsqrt(mean_square + EPSILON) * kv_gain[None, :]
    rope_part = rotate(projection[:, KV_RANK:], positions)
    return jnp.concatenate([normed, rope_part], -1).astype(jnp.bfloat16)


def update(running, group_queries, group_start, key_piece, key_start):
    query_count = group_queries.shape[0]
    key_count = key_piece.shape[0]

    def attend(current):
        top_score, weight_total, weighted = current
        scores = (
            jnp.einsum("qhc,kc->hqk", group_queries, key_piece, preferred_element_type=jnp.float32)
            * SCORE_SCALE
        )
        key_positions = jnp.arange(key_count, dtype=jnp.int32)
        query_positions = group_start + jnp.arange(query_count, dtype=jnp.int32)
        allowed = (key_positions[None, :] <= query_positions[:, None])[None]
        scores = jnp.where(allowed, scores, -1e30)
        new_max = jnp.maximum(top_score, jnp.max(scores, axis=-1))
        rescale = jnp.exp(top_score - new_max)
        weights = jnp.where(allowed, jnp.exp(scores - new_max[..., None]), 0.0)
        new_total = jnp.sum(weights, axis=-1)
        added_term = jnp.einsum(
            "hqk,kc->hqc",
            weights.astype(jnp.bfloat16),
            key_piece[:, :KV_RANK],
            preferred_element_type=jnp.float32,
        )
        return (new_max, new_total, added_term)

    return lax.cond(
        key_start <= group_start + query_count - 1, attend, lambda unchanged: unchanged, running
    )


def project(running, w_value):
    latent_out = (running[2] / running[1][..., None]).astype(jnp.bfloat16)
    projected = jnp.einsum("hqc,hcv->qhv", latent_out, w_value, preferred_element_type=jnp.float32)
    return projected.astype(jnp.bfloat16).reshape(projected.shape[0], -1)


def shards(hidden, w_kv_down, kv_gain, q_latent, q_rope, w_value):
    tok_rows = hidden.shape[0]
    heads_here = q_latent.shape[1]
    seq_index = lax.axis_index("seq")
    own_start = seq_index * tok_rows
    partial_value = jnp.dot(hidden, w_kv_down, preferred_element_type=jnp.float32)
    summed = of_everyone(partial_value, "tp")
    key_here = finish(summed, kv_gain, own_start + jnp.arange(tok_rows, dtype=jnp.int32))
    rope_query = rotate(
        q_rope.astype(jnp.float32).reshape(tok_rows, heads_here, ROPE),
        own_start + jnp.arange(tok_rows, dtype=jnp.int32),
    ).astype(jnp.bfloat16)
    queries = jnp.concatenate([q_latent, rope_query], -1)
    query_groups = ((queries, own_start),)

    def fresh_state(query_count):
        return (
            jnp.full((heads_here, query_count), -1e30, jnp.float32),
            jnp.zeros((heads_here, query_count), jnp.float32),
            jnp.zeros((heads_here, query_count, KV_RANK), jnp.float32),
        )

    fold_states = tuple((fresh_state(group[0].shape[0]) for group in query_groups))

    def absorb(running_all, key_piece, key_start):
        return tuple(
            (
                update(running, group[0], group[1], key_piece, key_start)
                for running, group in zip(running_all, query_groups)
            )
        )

    fold_states = absorb(
        fold_states, lax.all_gather(key_here, "seq", axis=0, tiled=True), jnp.int32(0)
    )
    results = [project(running, w_value) for running in fold_states]
    return results[0]


def solution(mesh):
    placed = (
        P("seq", "tp"),
        P("tp", None),
        P(),
        P("seq", "tp", None),
        P("seq", "tp"),
        P("tp", None, None),
    )
    return jax.shard_map(
        shards, mesh=mesh, in_specs=placed, out_specs=P("seq", "tp"), check_vma=False
    )
```

profile of v0, /device:TPU:1, one launch (start us, length us, event | category | flops | bytes accessed | tf_op | source)
XLA Modules:
  0.0 188.3 jit_solution(8439557678805121426)
XLA Ops:
  6.5 0.0 copy-start
  6.5 1.8 fusion.11
  8.4 0.0 copy-start.2
  8.4 1.6 broadcast_in_dim.44
  10.0 0.0 copy-start.1
  10.0 6.0 %all-to-all-start = ((f32[8,128,576]{1,2,0:T(8,128)}), f32[8,128,576]{1,2,0:T(8,128)S(1)}, u32[]{:S(2)}, u32[]{:S(2)}) async-start(f32[8,128,576]{1,2,0:T(8,128)} %broadcast_in_dim.44), calls=%async_computation | async-start | bytes 4718592 | tf_op jit(solution)/shard_map/all_to_all | solution.py:15
  16.0 0.0 all-gather.2.cloned.1.call-start
  16.0 34.1 %all-to-all-done = f32[8,128,576]{1,2,0:T(8,128)S(1)} async-done(((f32[8,128,576]{1,2,0:T(8,128)}), f32[8,128,576]{1,2,0:T(8,128)S(1)}, u32[]{:S(2)}, u32[]{:S(2)}) %all-to-all-start) | async-done | bytes 2359328 | tf_op jit(solution)/shard_map/all_to_all | solution.py:15
  50.2 0.8 reduce_sum.27
  51.0 1.0 multiply_reduce_fusion
  52.1 0.9 multiply_cosine_fusion
  52.9 0.0 copy-done.2
  52.9 1.1 multiply_convert_fusion
  54.0 0.7 pad_maximum_fusion.1
  54.7 0.0 all-gather.2.cloned.1.call-update
  54.7 0.0 copy-done.1
  54.7 0.1 copy.26
  54.8 1.9 %copy.27 = bf16[128,8,512]{0,2,1:T(8,128)(2,1)S(1)} copy(bf16[128,8,512]{2,1,0:T(8,128)(2,1)} %param.11) | data formatting | bytes 2097152 | tf_op args[3]
  56.9 1.1 pad_maximum_fusion
  58.0 88.2 %all-gather.2.cloned.1.call-done = bf16[4096,576]{0,1:T(8,128)(2,1)} async-done(((bf16[128,576]{0,1:T(8,128)(2,1)}), bf16[4096,576]{0,1:T(8,128)(2,1)}) %all-gather.2.cloned.1.call-update) | async-done | bytes 4718608 | tf_op jit(solution)/shard_map/all_gather | solution.py:122
  146.1 32.1 %conditional.1 = (f32[8,128]{1,0:T(8,128)S(1)}, f32[8,128,512]{2,1,0:T(8,128)}) conditional(s32[]{:T(128)} %convert_element_type.26, () %tuple.13, (s32[]{:T(128)}, bf16[4096,576]{0,1:T(8,128)(2,1)}, bf16[128,8,576]{0,2,1:T(8,128)(2,1)}) %tuple.14), branch_computations={%region_2.0_spmd, %region_3.6_spmd} | conditional | flops 9181854720 | bytes 74081296 | solution.py:78
  146.2 1.2 iota_compare_fusion
  147.3 7.6 %copy.28 = bf16[4096,576]{1,0:T(8,128)(2,1)} copy(bf16[4096,576]{0,1:T(8,128)(2,1)} %get-tuple-element.19) | data formatting | bytes 9437184 | tf_op jit(solution)/shard_map
  154.9 10.0 %fusion = (f32[8,128]{1,0:T(8,128)S(1)}, f32[4096,128,8]{1,0,2:T(8,128)S(1)}) fusion(pred[128,4096]{0,1:T(8,128)(4,1)} %iota_compare_fusion, bf16[128,8,576]{0,2,1:T(8,128)(2,1)} %get-tuple-element.13, bf16[4096,576]{0,1:T(8,128)(2,1)} %get-tuple-element.19), kind=kOutput, calls=%fused_computation.2 | convolution fusion | flops 4844420096 | bytes 23203840 | tf_op jit(solution)/shard_map/cond/branch_1_fun/qhc,kc->hqk/dot_general | solution.py:59
  164.9 8.4 %fusion.3 = f32[8,128,512]{2,1,0:T(8,128)} fusion(f32[4096,128,8]{1,0,2:T(8,128)S(1)} %get-tuple-element.22, f32[8,128]{1,0:T(8,128)S(1)} %broadcast_maximum_fusion, pred[128,4096]{0,1:T(8,128)(4,1)} %iota_compare_fusion, bf16[4096,576]{1,0:T(8,128)(2,1)} %copy.28), kind=kOutput, calls=%fused_computation.5 | convolution fusion | flops 4315938816 | bytes 23597056 | tf_op jit(solution)/shard_map/cond/branch_1_fun/hqk,kc->hqc/dot_general | solution.py:70
  173.4 4.9 %fusion.2 = f32[8,128]{1,0:T(8,128)S(1)} fusion(f32[4096,128,8]{1,0,2:T(8,128)S(1)} %get-tuple-element.22, f32[8,128]{1,0:T(8,128)S(1)} %broadcast_maximum_fusion, pred[128,4096]{0,1:T(8,128)(4,1)} %iota_compare_fusion), kind=kLoop, calls=%fused_computation.4 | loop fusion | flops 20970496 | bytes 17309696 | tf_op jit(solution)/shard_map/cond/branch_1_fun/reduce_sum | solution.py:69
  178.3 0.0 copy-done
  178.3 2.2 %convolution_convert_fusion = bf16[8,128,128]{1,2,0:T(8,128)(2,1)S(1)} fusion(bf16[8,512,128]{2,1,0:T(8,128)(2,1)S(1)} %copy-done, f32[8,128,512]{2,1,0:T(8,128)} %get-tuple-element.16, f32[8,128]{1,0:T(8,128)S(1)} %get-tuple-element.17), kind=kOutput, calls=%fused_computation.17 | convolution fusion | flops 135397376 | bytes 3411968 | tf_op jit(solution)/shard_map/hqc,hcv->qhv/dot_general | solution.py:85
  180.6 0.9 copy.30
  (6 shorter events, 0.1 us)
Async XLA Ops:
  6.5 171.8 %copy-start = (bf16[8,512,128]{2,1,0:T(8,128)(2,1)S(1)}, bf16[8,512,128]{2,1,0:T(8,128)(2,1)}, u32[]{:S(2)}) copy-start(bf16[8,512,128]{2,1,0:T(8,128)(2,1)} %param.13) | copy-start | bytes 3145732
  8.4 44.6 %copy-start.2 = (f32[512]{0:T(512)S(1)}, f32[512]{0:T(512)}, u32[]{:S(2)}) copy-start(f32[512]{0:T(512)} %param.10) | copy-start | bytes 6148
  10.0 44.8 %copy-start.1 = (bf16[128,512]{1,0:T(8,128)(2,1)S(1)}, bf16[128,512]{1,0:T(8,128)(2,1)}, u32[]{:S(2)}) copy-start(bf16[128,512]{1,0:T(8,128)(2,1)} %param.12) | copy-start | bytes 393220
  10.0 40.2 %all-to-all-start = ((f32[8,128,576]{1,2,0:T(8,128)}), f32[8,128,576]{1,2,0:T(8,128)S(1)}, u32[]{:S(2)}, u32[]{:S(2)}) async-start(f32[8,128,576]{1,2,0:T(8,128)} %broadcast_in_dim.44), calls=%async_computation | async-start | bytes 4718592 | tf_op jit(solution)/shard_map/all_to_all | solution.py:15
  16.0 130.2 %all-gather.2.cloned.1.call-start = ((), (), s32[]{:S(2)}) async-start(), calls=%async_computation.1 | async-start | bytes 4866048 | tf_op jit(solution)/shard_map/all_gather | solution.py:122
Sparse Core Ops, SparseCore 0:
  54.9 91.2 all-gather.1
where the time goes:
time: 189 us; the launch traced here: 188 us
  waiting for transfers between devices  122 us (65%)
  matrix products  22.5 us (12%)
  between operations  13.5 us (7%)
  local copies, waits for them, and re-layouts  12.1 us (6%)
  other arithmetic  11.8 us (6%)
  starting transfers between devices  6.03 us (3%)
    all_gather x1, waiting for transfers between devices, shards(): lax.all_gather(key_here, 'seq', axis=0, tiled=True)  88.2 us
    all_to_all x1, waiting for transfers between devices, from_everyone(): lax.all_to_all(jnp.broadcast_to(shard[None], (size, *shard.shape)), axis,...  34.1 us
    dot_general x1, matrix products, attend(): jnp.einsum('qhc,kc->hqk', group_queries, key_piece, preferred_element_typ...  9.97 us
    dot_general x1, matrix products, attend(): jnp.einsum('hqk,kc->hqc', weights.astype(jnp.bfloat16), key_piece[:, :KV_...  8.43 us
    another operation x1, local copies, waits for them, and re-layouts  7.63 us
    all_to_all x1, starting transfers between devices, from_everyone(): lax.all_to_all(jnp.broadcast_to(shard[None], (size, *shard.shape)), axis,...  5.99 us
    reduce_sum x1, other arithmetic, attend(): new_total = jnp.sum(weights, axis=-1)  4.93 us
  transfers between devices with their start and end apart: 2, of which 2 were waited for; matrix products, arithmetic and copies ran while one was open for 2% of the time, Pallas kernels for 0%

commit v1 on v0

--- a/solution.py
+++ b/solution.py
@@ -119,7 +119,11 @@
         )
 
     fold_states = absorb(
-        fold_states, lax.all_gather(key_here, "seq", axis=0, tiled=True), jnp.int32(0)
+        fold_states,
+        jnp.concatenate(
+            lax.all_to_all(jnp.stack([key_here] * lax.axis_size("seq")), "seq", 0, 0), axis=0
+        ),
+        jnp.int32(0),
     )
     results = [project(running, w_value) for running in fold_states]
     return results[0]

time: 189 us -> 206 us (1.090)
  waiting for transfers between devices: 122 us -> 139 us
  between operations: 13.5 us -> 0.12 us
  starting transfers between devices: 6.03 us -> 18.6 us
  local copies, waits for them, and re-layouts: 12.1 us -> 14.3 us
    all_to_all x0 -> x1, waiting for transfers between devices: none -> 105 us  [shards(): lax.all_to_all(jnp.stack([key_here] * lax.axis_size('seq')), 'seq', 0, 0)]
    all_gather x1 -> x0, waiting for transfers between devices: 88.2 us -> none  [shards(): lax.all_gather(key_here, 'seq', axis=0, tiled=True)]
    all_to_all x0 -> x1, starting transfers between devices: none -> 12.8 us  [shards(): lax.all_to_all(jnp.stack([key_here] * lax.axis_size('seq')), 'seq', 0, 0)]
    another operation x1 -> x2, local copies, waits for them, and re-layouts: 7.63 us -> 10.8 us
  transfers between devices with their start and end apart: 2 -> 2, of which waited for: 2 -> 2; matrix products, arithmetic and copies ran while one was open for 2% -> 1% of each run, Pallas kernels for 0% -> 0%
where the time goes in v1:
time: 206 us
  waiting for transfers between devices  139 us (67%)
  matrix products  22.3 us (11%)
  starting transfers between devices  18.6 us (9%)
  local copies, waits for them, and re-layouts  14.3 us (7%)
  other arithmetic  11.1 us (5%)
    all_to_all x1, waiting for transfers between devices, shards(): lax.all_to_all(jnp.stack([key_here] * lax.axis_size('seq')), 'seq', 0, 0)  105 us
    all_to_all x1, waiting for transfers between devices, from_everyone(): lax.all_to_all(jnp.broadcast_to(shard[None], (size, *shard.shape)), axis,...  34.2 us
    all_to_all x1, starting transfers between devices, shards(): lax.all_to_all(jnp.stack([key_here] * lax.axis_size('seq')), 'seq', 0, 0)  12.8 us
    dot_general x1, matrix products, attend(): jnp.einsum('qhc,kc->hqk', group_queries, key_piece, preferred_element_typ...  9.78 us
    dot_general x1, matrix products, attend(): jnp.einsum('hqk,kc->hqc', weights.astype(jnp.bfloat16), key_piece[:, :KV_...  8.44 us
    another operation x1, local copies, waits for them, and re-layouts  7.63 us
    all_to_all x1, starting transfers between devices, from_everyone(): lax.all_to_all(jnp.broadcast_to(shard[None], (size, *shard.shape)), axis,...  5.86 us
    reduce_sum x1, other arithmetic, attend(): new_total = jnp.sum(weights, axis=-1)  4.93 us
  transfers between devices with their start and end apart: 2, of which 2 were waited for; matrix products, arithmetic and copies ran while one was open for 1% of the time, Pallas kernels for 0%

profile of v1, /device:TPU:1, one launch (start us, length us, event | category | flops | bytes accessed | tf_op | source)
XLA Modules:
  0.0 205.8 jit_solution(16434107289466438274)
XLA Ops:
  0.0 0.0 copy-start
  0.0 1.8 fusion.9
  1.9 0.0 copy-start.3
  1.9 1.6 broadcast_in_dim.44
  3.4 5.9 %all-to-all-start = ((f32[8,128,576]{1,2,0:T(8,128)}), f32[8,128,576]{1,2,0:T(8,128)S(1)}, u32[]{:S(2)}, u32[]{:S(2)}) async-start(f32[8,128,576]{1,2,0:T(8,128)} %broadcast_in_dim.44), calls=%async_computation | async-start | bytes 4718592 | tf_op jit(solution)/shard_map/all_to_all | solution.py:15
  9.3 34.2 %all-to-all-done = f32[8,128,576]{1,2,0:T(8,128)S(1)} async-done(((f32[8,128,576]{1,2,0:T(8,128)}), f32[8,128,576]{1,2,0:T(8,128)S(1)}, u32[]{:S(2)}, u32[]{:S(2)}) %all-to-all-start) | async-done | bytes 2359328 | tf_op jit(solution)/shard_map/all_to_all | solution.py:15
  43.5 0.8 reduce_sum.27
  44.3 1.0 multiply_reduce_fusion
  45.4 0.9 multiply_cosine_fusion
  46.3 0.0 copy-done.3
  46.3 1.1 multiply_convert_fusion
  47.4 3.2 %stack.2 = bf16[32,128,576]{1,2,0:T(8,128)(2,1)} broadcast(bf16[128,576]{0,1:T(8,128)(2,1)S(1)} %pad_maximum_fusion.1), dimensions={1,2} | broadcast | bytes 4866048 | tf_op jit(solution)/shard_map/stack | solution.py:124
  50.6 0.0 copy-start.2
  50.6 0.0 copy-start.1
  50.6 12.8 %all-to-all-start.1 = ((bf16[32,128,576]{1,2,0:T(8,128)(2,1)}), bf16[32,128,576]{1,2,0:T(8,128)(2,1)}, u32[]{:S(2)}, u32[]{:S(2)}) async-start(bf16[32,128,576]{1,2,0:T(8,128)(2,1)} %stack.2), calls=%async_computation.1 | async-start | bytes 9437184 | tf_op jit(solution)/shard_map/all_to_all | solution.py:124
  63.3 0.0 copy-done.2
  63.4 0.1 copy.17
  63.5 0.0 copy-done.1
  63.5 1.0 copy.18
  64.5 1.1 pad_maximum_fusion
  65.7 105.1 %all-to-all-done.1 = bf16[32,128,576]{1,2,0:T(8,128)(2,1)} async-done(((bf16[32,128,576]{1,2,0:T(8,128)(2,1)}), bf16[32,128,576]{1,2,0:T(8,128)(2,1)}, u32[]{:S(2)}, u32[]{:S(2)}) %all-to-all-start.1) | async-done | bytes 4718624 | tf_op jit(solution)/shard_map/all_to_all | solution.py:124
  170.7 32.0 %conditional.1 = (f32[8,128]{1,0:T(8,128)S(1)}, f32[8,128,512]{2,1,0:T(8,128)}) conditional(s32[]{:T(128)} %convert_element_type.28, () %tuple.13, (s32[]{:T(128)}, bf16[32,128,576]{1,2,0:T(8,128)(2,1)}, bf16[128,8,576]{0,2,1:T(8,128)(2,1)}) %tuple.14), branch_computations={%region_2.0_spmd, %region_3.6_spmd} | conditional | flops 9181854720 | bytes 74081296 | solution.py:78
  170.7 1.2 iota_compare_fusion
  171.9 7.6 %copy.19 = bf16[32,128,576]{2,1,0:T(8,128)(2,1)} copy(bf16[32,128,576]{1,2,0:T(8,128)(2,1)} %get-tuple-element.20) | data formatting | bytes 9437184 | tf_op jit(solution)/shard_map
  179.5 9.8 %fusion = (f32[8,128]{1,0:T(8,128)S(1)}, f32[4096,128,8]{1,0,2:T(8,128)S(1)}) fusion(pred[128,4096]{0,1:T(8,128)(4,1)} %iota_compare_fusion, bf16[4096,576,1]{1,0,2:T(8,128)(2,1)} %bitcast.26, bf16[128,8,576]{0,2,1:T(8,128)(2,1)} %get-tuple-element.14), kind=kOutput, calls=%fused_computation.2 | convolution fusion | flops 4844420096 | bytes 23203840 | tf_op jit(solution)/shard_map/cond/branch_1_fun/qhc,kc->hqk/dot_general | solution.py:59
  189.3 8.4 %fusion.3 = f32[8,128,512]{2,1,0:T(8,128)} fusion(f32[4096,128,8]{1,0,2:T(8,128)S(1)} %get-tuple-element.23, f32[8,128]{1,0:T(8,128)S(1)} %broadcast_maximum_fusion, pred[128,4096]{0,1:T(8,128)(4,1)} %iota_compare_fusion, bf16[4096,576]{1,0:T(8,128)(2,1)} %bitcast.27), kind=kOutput, calls=%fused_computation.5 | convolution fusion | flops 4315938816 | bytes 23597056 | tf_op jit(solution)/shard_map/cond/branch_1_fun/hqk,kc->hqc/dot_general | solution.py:70
  197.8 4.9 %fusion.2 = f32[8,128]{1,0:T(8,128)S(1)} fusion(f32[4096,128,8]{1,0,2:T(8,128)S(1)} %get-tuple-element.23, f32[8,128]{1,0:T(8,128)S(1)} %broadcast_maximum_fusion, pred[128,4096]{0,1:T(8,128)(4,1)} %iota_compare_fusion), kind=kLoop, calls=%fused_computation.4 | loop fusion | flops 20970496 | bytes 17309696 | tf_op jit(solution)/shard_map/cond/branch_1_fun/reduce_sum | solution.py:69
  202.7 0.0 copy-done
  202.7 2.2 %convolution_convert_fusion = bf16[8,128,128]{1,2,0:T(8,128)(2,1)S(1)} fusion(bf16[8,512,128]{2,1,0:T(8,128)(2,1)S(1)} %copy-done, f32[8,128,512]{2,1,0:T(8,128)} %get-tuple-element.17, f32[8,128]{1,0:T(8,128)S(1)} %get-tuple-element.18), kind=kOutput, calls=%fused_computation.15 | convolution fusion | flops 135397376 | bytes 3411968 | tf_op jit(solution)/shard_map/hqc,hcv->qhv/dot_general | solution.py:85
  204.9 0.9 copy.21
  (7 shorter events, 0.1 us)
Async XLA Ops:
  0.0 202.7 %copy-start = (bf16[8,512,128]{2,1,0:T(8,128)(2,1)S(1)}, bf16[8,512,128]{2,1,0:T(8,128)(2,1)}, u32[]{:S(2)}) copy-start(bf16[8,512,128]{2,1,0:T(8,128)(2,1)} %param.13) | copy-start | bytes 3145732
  1.9 44.4 %copy-start.3 = (f32[512]{0:T(512)S(1)}, f32[512]{0:T(512)}, u32[]{:S(2)}) copy-start(f32[512]{0:T(512)} %param.10) | copy-start | bytes 6148
  3.4 40.1 %all-to-all-start = ((f32[8,128,576]{1,2,0:T(8,128)}), f32[8,128,576]{1,2,0:T(8,128)S(1)}, u32[]{:S(2)}, u32[]{:S(2)}) async-start(f32[8,128,576]{1,2,0:T(8,128)} %broadcast_in_dim.44), calls=%async_computation | async-start | bytes 4718592 | tf_op jit(solution)/shard_map/all_to_all | solution.py:15
  50.6 12.8 %copy-start.2 = (bf16[128,512]{1,0:T(8,128)(2,1)S(1)}, bf16[128,512]{1,0:T(8,128)(2,1)}, u32[]{:S(2)}) copy-start(bf16[128,512]{1,0:T(8,128)(2,1)} %param.12) | copy-start | bytes 393220
  50.6 12.9 %copy-start.1 = (bf16[128,8,512]{2,1,0:T(8,128)(2,1)S(1)}, bf16[128,8,512]{2,1,0:T(8,128)(2,1)}, u32[]{:S(2)}) copy-start(bf16[128,8,512]{2,1,0:T(8,128)(2,1)} %param.11) | copy-start | bytes 3145732
  50.6 120.1 %all-to-all-start.1 = ((bf16[32,128,576]{1,2,0:T(8,128)(2,1)}), bf16[32,128,576]{1,2,0:T(8,128)(2,1)}, u32[]{:S(2)}, u32[]{:S(2)}) async-start(bf16[32,128,576]{1,2,0:T(8,128)(2,1)} %stack.2), calls=%async_computation.1 | async-start | bytes 9437184 | tf_op jit(solution)/shard_map/all_to_all | solution.py:124
